TPU v7x, 32 devices: a whole 2x2x4 slice. The times are simulated.
32 devices in a mesh: dp: 4 (over z), row: 2 (over core), col: 4 (over y, x).
Axes of the slice: x: 2, y: 2, z: 4, core: 2. Of those that a mesh axis runs over, the one named last changes fastest.
Arguments:
- features: bfloat16 [2048, 4096], P(('dp', 'row')), may hold values from -6 to 6
- w_in: bfloat16 [4096, 4096], P('row', 'col'), may hold values from -0.09375 to 0.09375
- w_out: bfloat16 [4096, 1024], P('col'), may hold values from -0.09375 to 0.09375
- captions: bfloat16 [2048, 1024], P(('dp', 'row', 'col')), may hold values from -6 to 6
- positive: int32 [2048], P(('dp', 'row')), may hold values from 0 to 2047, each once
Outputs:
- fig_terms: float32 [2048], P(('dp', 'row'))
- cap_terms: float32 [2048], P(('dp', 'row', 'col'))
- grad_w_in: float32 [4096, 4096], P(('dp', 'row'), 'col')
- grad_w_out: float32 [4096, 1024], P('col', ('dp', 'row'))
Inputs may be any that keep to these rules, and one draw needn't show every extreme that they name: positive is a permutation: every caption is the match of exactly one figure.
All inputs are finite; a program needn't handle non-finite values.
Results may differ from a plain program's by a relative error of at most 0.0053.
Values may be sent and summed in bfloat16 or wider, within the bound.
A program may use at most 128 MiB of HBM per device.

v0:
```python
import jax
import jax.numpy as jnp
from jax import lax
from jax.sharding import PartitionSpec as P

SCALE = 50.0
EPS = 1e-06


def gelu_back(pre, grad):
    return jax.vjp(jax.nn.gelu, pre)[1](grad)[0]


def on_device(features, w_in, w_out, captions, positive):
    group = ("dp", "row")
    every = ("dp", "row", "col")
    f32 = jnp.float32
    slices = lax.all_to_all(features, group, 1, 0, tiled=True)
    cap32 = captions.astype(f32)
    chat_local = (cap32 * lax.rsqrt(jnp.sum(cap32 * cap32, axis=1, keepdims=True) + EPS)).astype(
        jnp.bfloat16
    )
    chat = lax.all_gather(chat_local, every, axis=0, tiled=True)
    pre = jnp.dot(
        features, lax.all_gather(w_in, "row", axis=0, tiled=True), preferred_element_type=f32
    )
    hidden = jax.nn.gelu(pre).astype(jnp.bfloat16)
    part = jnp.dot(hidden, w_out, preferred_element_type=f32)
    emb = lax.psum_scatter(part, "col", scatter_dimension=0, tiled=True)
    mine = emb.shape[0]
    inv = lax.rsqrt(jnp.sum(emb * emb, axis=1, keepdims=True) + EPS)
    fhat = emb * inv
    fhat_b = fhat.astype(jnp.bfloat16)
    logits = SCALE * lax.dot_general(
        fhat_b, chat, (((1,), (1,)), ((), ())), preferred_element_type=f32
    )
    col = lax.axis_index("col")
    places = lax.dynamic_slice_in_dim(positive, col * mine, mine, 0)
    colids = jnp.arange(chat.shape[0], dtype=jnp.int32)
    mask = (places[:, None] == colids[None, :]).astype(f32)
    expo = jnp.exp(logits)
    picked = mask * logits
    rowsum, rowpos = (jnp.sum(expo, axis=1), jnp.sum(picked, axis=1))
    colsum, colpos = lax.psum((jnp.sum(expo, axis=0), jnp.sum(picked, axis=0)), every)
    fig_terms = lax.all_gather(jnp.log(rowsum) - rowpos, "col", axis=0, tiled=True)
    capdev = captions.shape[0]
    place = (lax.axis_index("dp") * lax.axis_size("row") + lax.axis_index("row")) * lax.axis_size(
        "col"
    ) + col
    cap_terms = lax.dynamic_slice_in_dim(jnp.log(colsum) - colpos, place * capdev, capdev, 0)
    dlog = (expo / rowsum[:, None] + expo / colsum[None, :] - 2.0 * mask).astype(jnp.bfloat16)
    dfhat = SCALE * jnp.dot(dlog, chat, preferred_element_type=f32)
    demb = ((dfhat - fhat * jnp.sum(fhat * dfhat, axis=1, keepdims=True)) * inv).astype(
        jnp.bfloat16
    )
    demb = lax.all_gather(demb, "col", axis=0, tiled=True)
    dh = lax.dot_general(demb, w_out, (((1,), (1,)), ((), ())), preferred_element_type=f32)
    dpre = gelu_back(pre, dh).astype(jnp.bfloat16)
    dpre_all = lax.all_gather(dpre, group, axis=0, tiled=True)
    head_term = lax.dot_general(hidden, demb, (((0,), (0,)), ((), ())), preferred_element_type=f32)
    grad_w_out = lax.psum_scatter(head_term, group, scatter_dimension=1, tiled=True)
    grad_w_in = lax.dot_general(
        slices, dpre_all, (((0,), (0,)), ((), ())), preferred_element_type=f32
    )
    return (fig_terms, cap_terms, grad_w_in, grad_w_out)


def solution(mesh):
    placed = (
        P(("dp", "row"), None),
        P("row", "col"),
        P("col", None),
        P(("dp", "row", "col"), None),
        P(("dp", "row")),
    )
    return jax.shard_map(
        on_device,
        mesh=mesh,
        in_specs=placed,
        out_specs=(
            P(("dp", "row")),
            P(("dp", "row", "col")),
            P(("dp", "row"), "col"),
            P("col", ("dp", "row")),
        ),
        check_vma=False,
    )
```

profile of v0, /device:TPU:0, one launch (start us, length us, event | category | flops | bytes accessed | tf_op | source)
XLA Modules:
  0.0 310.4 jit_solution(15779341503108276041)
XLA Ops:
  8.1 0.7 all-gather.4.cloned.1.call-update
  8.8 24.2 %all-gather.4.cloned.1.call-done = bf16[4096,1024]{1,0:T(8,128)(2,1)} async-done(((bf16[2048,1024]{1,0:T(8,128)(2,1)}), bf16[4096,1024]{1,0:T(8,128)(2,1)}) %all-gather.4.cloned.1.call-update) | async-done | bytes 8388624 | tf_op jit(solution)/shard_map/all_gather | solution.py:25
  33.0 6.3 %fusion.22 = f32[256,1024]{1,0:T(8,128)S(1)} fusion(bf16[256,4096]{1,0:T(8,128)(2,1)} %param.5, bf16[4096,1024]{1,0:T(8,128)(2,1)} %all-gather.4.cloned.1.call-done), kind=kOutput, calls=%fused_computation.43 | convolution fusion | flops 2147483648 | bytes 11534336 | tf_op jit(solution)/shard_map/dot_general | solution.py:24
  39.3 1.1 copy-done.2
  40.4 1.8 fusion.21
  42.2 0.0 all-gather.6.cloned.1.call-start
  42.3 0.1 fusion.10
  42.4 0.8 fusion.11
  43.2 0.0 all-gather.8.cloned.1.call-start
  43.3 0.1 dynamic_slice.6
  43.4 28.3 %reduce-scatter.3.cloned.1.call-done = f32[64,1024]{1,0:T(8,128)} async-done(((f32[256,1024]{1,0:T(8,128)}), f32[64,1024]{1,0:T(8,128)}) %reduce-scatter.3.cloned.1.call-update) | async-done | bytes 262160 | tf_op jit(solution)/shard_map/reduce_scatter | solution.py:29
  71.6 1.1 multiply_reduce_fusion.1
  72.7 36.8 %all-gather.6.cloned.1.call-done = bf16[2048,1024]{1,0:T(8,128)(2,1)} async-done(((bf16[64,1024]{1,0:T(8,128)(2,1)}), bf16[2048,1024]{1,0:T(8,128)(2,1)}) %all-gather.6.cloned.1.call-update) | async-done | bytes 4194320 | tf_op jit(solution)/shard_map/all_gather | solution.py:23
  109.5 3.9 %fusion.8 = (f32[2048]{0:T(1024)S(1)}, f32[64]{0:T(128)S(1)}, f32[2048]{0:T(1024)S(1)}, f32[64]{0:T(128)S(1)}, f32[64,2048]{1,0:T(8,128)S(1)}) fusion(s32[64]{0:T(128)S(1)} %dynamic_slice.6, bf16[2048,1024]{1,0:T(8,128)(2,1)} %all-gather.6.cloned.1.call-done, f32[64,1024]{1,0:T(8,128)} %reduce-scatter.3.cloned.1.call-done, f32[64]{0:T(128)S(1)} %add_rsqrt_fusion.1), kind=kOutput, calls=%fused_computation.16 | convolution fusion | flops 269479808 | bytes 4998144 | tf_op jit(solution)/shard_map/dot_general | solution.py:34
  113.4 39.3 %all-reduce.1 = (f32[2048]{0:T(1024)S(1)}, f32[2048]{0:T(1024)S(1)}) all-reduce(f32[2048]{0:T(1024)S(1)} %get-tuple-element.16, f32[2048]{0:T(1024)S(1)} %get-tuple-element.18), channel_id=1, replica_groups=mesh['dp'=4,'row'=2,'col'=4] {'dp','row','col'}, use_global_device_ids=true, to_apply=%region_8.0 | all-reduce | flops 4096 | bytes 32768 | tf_op jit(solution)/shard_map/psum | solution.py:44
  152.7 3.3 %multiply_reduce_fusion = (f32[64]{0:T(128)S(1)}, f32[64,1024]{1,0:T(8,128)S(1)}) fusion(f32[64,1024]{1,0:T(8,128)S(1)} %copy-done.1, f32[64]{0:T(128)S(1)} %add_rsqrt_fusion.1, bf16[2048,1024]{1,0:T(8,128)(2,1)} %all-gather.6.cloned.1.call-done, f32[64,2048]{1,0:T(8,128)S(1)} %get-tuple-element.22, f32[2048]{0:T(1024)S(1)} %get-tuple-element.21, ...), kind=kOutput, calls=%fused_computation.25 | convolution fusion | flops 269615040 | bytes 5252096 | tf_op jit(solution)/shard_map/dot_general | solution.py:52
  156.0 0.1 multiply_convert_fusion.1
  156.1 11.6 %all_gather.18 = bf16[256,1024]{1,0:T(8,128)(2,1)S(1)} all-gather(bf16[64,1024]{1,0:T(8,128)(2,1)S(1)} %multiply_convert_fusion.1), channel_id=1, replica_groups=mesh['dp'=4,'row'=2,'col'=4] {'col'}, dimensions={0}, use_global_device_ids=true | all-gather | bytes 655360 | tf_op jit(solution)/shard_map/all_gather | solution.py:56
  167.7 2.1 fusion.6
  169.8 0.0 reduce-scatter.5.cloned.1.call-start
  169.9 4.0 %fusion.20 = f32[1024,1024]{1,0:T(8,128)} fusion(bf16[256,1024]{1,0:T(8,128)(2,1)S(1)} %all_gather.18, f32[256,1024]{1,0:T(8,128)} %copy-done.2), kind=kOutput, calls=%fused_computation.41 | convolution fusion | flops 539230208 | bytes 5767168 | tf_op jit(solution)/shard_map/dot_general | solution.py:60
  173.9 4.1 %copy.11 = bf16[256,4096]{0,1:T(8,128)(2,1)} copy(bf16[256,4096]{1,0:T(8,128)(2,1)} %param.5) | data formatting | bytes 4194304 | tf_op args[0]
  178.1 4.5 %all-to-all-start = ((bf16[256,8,512]{0,2,1:T(8,128)(2,1)}), bf16[256,8,512]{0,2,1:T(8,128)(2,1)}, u32[]{:S(2)}, u32[]{:S(2)}) async-start(bf16[256,8,512]{0,2,1:T(8,128)(2,1)} %bitcast.16), calls=%async_computation.1 | async-start | bytes 4194304 | tf_op jit(solution)/shard_map/all_to_all | solution.py:18
  182.6 0.6 dynamic-slice
  183.8 74.7 %all-to-all-done = bf16[256,8,512]{0,2,1:T(8,128)(2,1)} async-done(((bf16[256,8,512]{0,2,1:T(8,128)(2,1)}), bf16[256,8,512]{0,2,1:T(8,128)(2,1)}, u32[]{:S(2)}, u32[]{:S(2)}) %all-to-all-start) | async-done | bytes 2097184 | tf_op jit(solution)/shard_map/all_to_all | solution.py:18
  258.5 4.0 %copy.12 = bf16[8,256,512]{2,1,0:T(8,128)(2,1)} copy(bf16[8,256,512]{1,2,0:T(8,128)(2,1)} %bitcast.2) | data formatting | bytes 4194304 | tf_op jit(solution)/shard_map/all_to_all | solution.py:18
  262.5 0.1 subtract_dynamic-update-slice_fusion
  262.6 10.5 %all-reduce = f32[256]{0:T(256)} all-reduce(f32[256]{0:T(256)S(1)} %subtract_dynamic-update-slice_fusion), channel_id=1, replica_groups=mesh['dp'=4,'row'=2,'col'=4] {'col'}, use_global_device_ids=true, to_apply=%add | all-reduce | flops 256 | bytes 2048
  273.1 0.6 dynamic-slice_subtract_fusion
  273.7 6.7 %convolution_bitcast_fusion = f32[512,1024]{0,1:T(8,128)} fusion(bf16[2048,1024]{1,0:T(8,128)(2,1)} %all-gather.8.cloned.1.call-done, bf16[2048,512]{1,0:T(8,128)(2,1)} %bitcast.17), kind=kOutput, calls=%fused_computation.1 | convolution fusion | flops 2147483648 | bytes 8388608 | tf_op jit(solution)/shard_map/dot_general | solution.py:62
  280.4 2.9 copy.13
  283.3 19.6 %reduce-scatter.5.cloned.1.call-done = f32[1024,128]{1,0:T(8,128)} async-done(((f32[1024,1024]{1,0:T(8,128)}), f32[1024,128]{1,0:T(8,128)}) %reduce-scatter.5.cloned.1.call-update) | async-done | bytes 524304 | tf_op jit(solution)/shard_map/reduce_scatter | solution.py:61
  (23 shorter events, 0.2 us)
Async XLA Ops:
  8.0 32.4 %copy-start = (bf16[1024,1024]{1,0:T(8,128)(2,1)S(1)}, bf16[1024,1024]{1,0:T(8,128)(2,1)}, u32[]{:S(2)}) copy-start(bf16[1024,1024]{1,0:T(8,128)(2,1)} %param.7) | copy-start | bytes 6291460
  8.0 25.0 %all-gather.4.cloned.1.call-start = ((), (), s32[]{:S(2)}) async-start(), calls=%async_computation.3 | async-start | bytes 12582912 | tf_op jit(solution)/shard_map/all_gather | solution.py:25
  8.7 62.9 %reduce-scatter.3.cloned.1.call-start = ((), (), s32[]{:S(2)}) async-start(), calls=%async_computation.4 | async-start | bytes 1310720 | tf_op jit(solution)/shard_map/reduce_scatter | solution.py:29
  39.3 1.1 copy-start.2
  40.4 1.9 copy-start.4
  40.4 2.9 copy-start.5
  42.2 67.3 %all-gather.6.cloned.1.call-start = ((), (), s32[]{:S(2)}) async-start(), calls=%async_computation.5 | async-start | bytes 4325376 | tf_op jit(solution)/shard_map/all_gather | solution.py:23
  43.2 230.5 %all-gather.8.cloned.1.call-start = ((), (), s32[]{:S(2)}) async-start(), calls=%async_computation.6 | async-start | bytes 4718592 | tf_op jit(solution)/shard_map/all_gather | solution.py:59
  72.7 80.0 %copy-start.1 = (f32[64,1024]{1,0:T(8,128)S(1)}, f32[64,1024]{1,0:T(8,128)}, u32[]{:S(2)}) copy-start(f32[64,1024]{1,0:T(8,128)} %reduce-scatter.3.cloned.1.call-done) | copy-start | bytes 786436
  152.7 15.0 %copy-start.3 = (f32[256,1024]{1,0:T(8,128)S(1)}, f32[256,1024]{1,0:T(8,128)}, u32[]{:S(2)}) copy-start(f32[256,1024]{1,0:T(8,128)} %copy-done.2) | copy-start | bytes 3145732
  169.8 133.0 %reduce-scatter.5.cloned.1.call-start = ((), (), s32[]{:S(2)}) async-start(), calls=%async_computation.7 | async-start | bytes 4718592 | tf_op jit(solution)/shard_map/reduce_scatter | solution.py:61
  178.1 4.5 %copy-start.6 = (u32[32]{0:T(128)S(1)}, u32[32]{0:T(128)}, u32[]{:S(2)}) copy-start(u32[32]{0:T(128)} %constant.49) | copy-start | bytes 388
  178.1 80.4 %all-to-all-start = ((bf16[256,8,512]{0,2,1:T(8,128)(2,1)}), bf16[256,8,512]{0,2,1:T(8,128)(2,1)}, u32[]{:S(2)}, u32[]{:S(2)}) async-start(bf16[256,8,512]{0,2,1:T(8,128)(2,1)} %bitcast.16), calls=%async_computation.1 | async-start | bytes 4194304 | tf_op jit(solution)/shard_map/all_to_all | solution.py:18
Sparse Core Ops, SparseCore 0:
  10.4 22.5 all-gather.3
  42.4 29.2 reduce-scatter.2
Sparse Core Ops, SparseCore 1:
  46.2 63.3 all-gather.5
  169.9 81.1 all-gather.7
  253.9 48.9 reduce-scatter.4
where the time goes:
time: 311 us; the launch traced here: 310 us
  waiting for transfers between devices  184 us (59%)
  blocking collectives  61.4 us (20%)
  matrix products  28.1 us (9%)
  between operations  16.4 us (5%)
  local copies, waits for them, and re-layouts  12.8 us (4%)
  starting transfers between devices  4.7 us (2%)
    all_to_all x1, waiting for transfers between devices, on_device(): slices = lax.all_to_all(features, group, 1, 0, tiled=True)  74.7 us
    psum x1, blocking collectives, on_device(): lax.psum((jnp.sum(expo, axis=0), jnp.sum(picked, axis=0)), every)  39.3 us
    all_gather x1, waiting for transfers between devices, on_device(): chat = lax.all_gather(chat_local, every, axis=0, tiled=True)  36.8 us
    reduce_scatter x1, waiting for transfers between devices, on_device(): emb = lax.psum_scatter(part, 'col', scatter_dimension=0, tiled=True)  28.3 us
    all_gather x1, waiting for transfers between devices, on_device(): lax.all_gather(w_in, 'row', axis=0, tiled=True)  24.2 us
    reduce_scatter x1, waiting for transfers between devices, on_device(): lax.psum_scatter(head_term, group, scatter_dimension=1, tiled=True)  19.6 us
    all_gather x1, blocking collectives, on_device(): demb = lax.all_gather(demb, 'col', axis=0, tiled=True)  11.6 us
    unnamed x1, blocking collectives  10.5 us
  transfers between devices with their start and end apart: 6, of which 5 were waited for; matrix products, arithmetic and copies ran while one was open for 8% of the time, Pallas kernels for 0%

commit v1 on v0

--- a/solution.py
+++ b/solution.py
@@ -53,7 +53,12 @@
     demb = ((dfhat - fhat * jnp.sum(fhat * dfhat, axis=1, keepdims=True)) * inv).astype(
         jnp.bfloat16
     )
-    demb = lax.all_gather(demb, "col", axis=0, tiled=True)
+    ring = [demb]
+    for hop in range(3):
+        ring.append(lax.ppermute(ring[-1], "col", [(dev, (dev + 1) % 4) for dev in range(4)]))
+    demb = jnp.roll(
+        jnp.concatenate(ring[::-1], axis=0), (lax.axis_index("col") + 1) * ring[0].shape[0], axis=0
+    )
     dh = lax.dot_general(demb, w_out, (((1,), (1,)), ((), ())), preferred_element_type=f32)
     dpre = gelu_back(pre, dh).astype(jnp.bfloat16)
     dpre_all = lax.all_gather(dpre, group, axis=0, tiled=True)

time: 311 us -> 322 us (1.035)
  waiting for transfers between devices: 184 us -> 201 us
  blocking collectives: 61.4 us -> 49.7 us
    ppermute x0 -> x3, waiting for transfers between devices: none -> 15.4 us  [on_device(): lax.ppermute(ring[-1], 'col', [(dev, (dev + 1) % 4) for dev in range(4)])]
    all_gather x1 -> x0, blocking collectives: 11.6 us -> none  [on_device(): demb = lax.all_gather(demb, 'col', axis=0, tiled=True)]
    unnamed x18 -> x25, local copies, waits for them, and re-layouts: 8.7 us -> 10.5 us
  transfers between devices with their start and end apart: 6 -> 9, of which waited for: 5 -> 8; matrix products, arithmetic and copies ran while one was open for 8% -> 8% of each run, Pallas kernels for 0% -> 0%
where the time goes in v1:
time: 322 us
  waiting for transfers between devices  201 us (62%)
  blocking collectives  49.7 us (15%)
  matrix products  28.8 us (9%)
  between operations  16.5 us (5%)
  local copies, waits for them, and re-layouts  14.5 us (5%)
  starting transfers between devices  7.76 us (2%)
  other arithmetic  3.44 us (1%)
    all_to_all x1, waiting for transfers between devices, on_device(): slices = lax.all_to_all(features, group, 1, 0, tiled=True)  75.2 us
    psum x1, blocking collectives, on_device(): lax.psum((jnp.sum(expo, axis=0), jnp.sum(picked, axis=0)), every)  39.3 us
    all_gather x1, waiting for transfers between devices, on_device(): chat = lax.all_gather(chat_local, every, axis=0, tiled=True)  36.8 us
    reduce_scatter x1, waiting for transfers between devices, on_device(): emb = lax.psum_scatter(part, 'col', scatter_dimension=0, tiled=True)  28.3 us
    all_gather x1, waiting for transfers between devices, on_device(): lax.all_gather(w_in, 'row', axis=0, tiled=True)  24.2 us
    reduce_scatter x1, waiting for transfers between devices, on_device(): lax.psum_scatter(head_term, group, scatter_dimension=1, tiled=True)  20.2 us
    ppermute x3, waiting for transfers between devices, on_device(): lax.ppermute(ring[-1], 'col', [(dev, (dev + 1) % 4) for dev in range(4)])  15.4 us
    unnamed x25, local copies, waits for them, and re-layouts  10.5 us
  transfers between devices with their start and end apart: 9, of which 8 were waited for; matrix products, arithmetic and copies ran while one was open for 8% of the time, Pallas kernels for 0%

profile of v1, /device:TPU:0, one launch (start us, length us, event | category | flops | bytes accessed | tf_op | source)
XLA Modules:
  0.0 321.6 jit_solution(14481256050838217552)
XLA Ops:
  8.1 0.7 all-gather.4.cloned.1.call-update
  8.8 24.2 %all-gather.4.cloned.1.call-done = bf16[4096,1024]{1,0:T(8,128)(2,1)} async-done(((bf16[2048,1024]{1,0:T(8,128)(2,1)}), bf16[4096,1024]{1,0:T(8,128)(2,1)}) %all-gather.4.cloned.1.call-update) | async-done | bytes 8388624 | tf_op jit(solution)/shard_map/all_gather | solution.py:25
  33.0 6.3 %fusion.29 = f32[256,1024]{1,0:T(8,128)S(1)} fusion(bf16[256,4096]{1,0:T(8,128)(2,1)} %param.5, bf16[4096,1024]{1,0:T(8,128)(2,1)} %all-gather.4.cloned.1.call-done), kind=kOutput, calls=%fused_computation.56 | convolution fusion | flops 2147483648 | bytes 11534336 | tf_op jit(solution)/shard_map/dot_general | solution.py:24
  39.4 1.8 fusion.28
  41.2 0.1 fusion.16
  41.4 0.8 fusion.17
  42.3 28.3 %reduce-scatter.3.cloned.1.call-done = f32[64,1024]{1,0:T(8,128)} async-done(((f32[256,1024]{1,0:T(8,128)}), f32[64,1024]{1,0:T(8,128)}) %reduce-scatter.3.cloned.1.call-update) | async-done | bytes 262160 | tf_op jit(solution)/shard_map/reduce_scatter | solution.py:29
  70.6 1.1 multiply_reduce_fusion.1
  71.7 36.8 %all-gather.6.cloned.1.call-done = bf16[2048,1024]{1,0:T(8,128)(2,1)} async-done(((bf16[64,1024]{1,0:T(8,128)(2,1)}), bf16[2048,1024]{1,0:T(8,128)(2,1)}) %all-gather.6.cloned.1.call-update) | async-done | bytes 4194320 | tf_op jit(solution)/shard_map/all_gather | solution.py:23
  108.5 4.6 %fusion.8 = (f32[2048]{0:T(1024)S(1)}, f32[64]{0:T(128)S(1)}, f32[2048]{0:T(1024)S(1)}, f32[64]{0:T(128)S(1)}, f32[64,2048]{1,0:T(8,128)}) fusion(s32[64]{0:T(128)S(1)} %dynamic_slice.10, bf16[2048,1024]{1,0:T(8,128)(2,1)} %all-gather.6.cloned.1.call-done, f32[64,1024]{1,0:T(8,128)} %reduce-scatter.3.cloned.1.call-done, f32[64]{0:T(128)S(1)} %add_rsqrt_fusion.1), kind=kOutput, calls=%fused_computation.16 | convolution fusion | flops 269479808 | bytes 4998144 | tf_op jit(solution)/shard_map/dot_general | solution.py:34
  113.1 39.3 %all-reduce.1 = (f32[2048]{0:T(1024)}, f32[2048]{0:T(1024)S(1)}) all-reduce(f32[2048]{0:T(1024)S(1)} %get-tuple-element.16, f32[2048]{0:T(1024)S(1)} %get-tuple-element.18), channel_id=1, replica_groups=mesh['dp'=4,'row'=2,'col'=4] {'dp','row','col'}, use_global_device_ids=true, to_apply=%region_8.0 | all-reduce | flops 4096 | bytes 32768 | tf_op jit(solution)/shard_map/psum | solution.py:44
  152.4 3.4 %multiply_reduce_fusion = (f32[64]{0:T(128)S(1)}, f32[64,1024]{1,0:T(8,128)S(1)}) fusion(f32[64,1024]{1,0:T(8,128)S(1)} %copy-done.1, f32[64]{0:T(128)S(1)} %add_rsqrt_fusion.1, bf16[2048,1024]{1,0:T(8,128)(2,1)} %all-gather.6.cloned.1.call-done, f32[64,2048]{1,0:T(8,128)} %get-tuple-element.22, f32[2048]{0:T(1024)S(1)} %get-tuple-element.21, ...), kind=kOutput, calls=%fused_computation.29 | convolution fusion | flops 269615040 | bytes 5252096 | tf_op jit(solution)/shard_map/dot_general | solution.py:52
  155.9 2.3 collective-permute-start
  158.2 4.2 %collective-permute-done = bf16[64,1024]{1,0:T(8,128)(2,1)S(1)} collective-permute-done((bf16[64,1024]{1,0:T(8,128)(2,1)S(1)}, bf16[64,1024]{1,0:T(8,128)(2,1)S(1)}, u32[]{:S(2)}, u32[]{:S(2)}) %collective-permute-start) | collective-permute-done | bytes 131104 | tf_op jit(solution)/shard_map/ppermute | solution.py:58
  162.5 0.7 collective-permute-start.1
  163.2 5.2 %collective-permute-done.1 = bf16[64,1024]{1,0:T(8,128)(2,1)S(1)} collective-permute-done((bf16[64,1024]{1,0:T(8,128)(2,1)S(1)}, bf16[64,1024]{1,0:T(8,128)(2,1)S(1)}, u32[]{:S(2)}, u32[]{:S(2)}) %collective-permute-start.1) | collective-permute-done | bytes 131104 | tf_op jit(solution)/shard_map/ppermute | solution.py:58
  168.4 6.0 %collective-permute-done.2 = bf16[64,1024]{1,0:T(8,128)(2,1)} collective-permute-done((bf16[64,1024]{1,0:T(8,128)(2,1)S(1)}, bf16[64,1024]{1,0:T(8,128)(2,1)}, u32[]{:S(2)}, u32[]{:S(2)}) %collective-permute-start.2) | collective-permute-done | bytes 131104 | tf_op jit(solution)/shard_map/ppermute | solution.py:58
  174.4 0.9 constant_dynamic-update-slice_fusion.7
  175.4 0.9 constant_dynamic-update-slice_fusion.3
  176.4 1.0 copy-done.3
  177.3 2.1 fusion.6
  179.5 3.9 %fusion.10 = f32[1024,1024]{1,0:T(8,128)} fusion(bf16[512,1024]{1,0:T(8,128)(2,1)} %copy-done.3, s32[]{:T(128)S(6)} %select_n.22, f32[256,1024]{1,0:T(8,128)S(1)} %fusion.29), kind=kOutput, calls=%fused_computation.20 | convolution fusion | flops 539230208 | bytes 5767172 | tf_op jit(solution)/shard_map/dot_general | solution.py:65
  183.4 4.1 %copy.11 = bf16[256,4096]{0,1:T(8,128)(2,1)} copy(bf16[256,4096]{1,0:T(8,128)(2,1)} %param.5) | data formatting | bytes 4194304 | tf_op args[0]
  187.5 4.5 %all-to-all-start = ((bf16[256,8,512]{0,2,1:T(8,128)(2,1)}), bf16[256,8,512]{0,2,1:T(8,128)(2,1)}, u32[]{:S(2)}, u32[]{:S(2)}) async-start(bf16[256,8,512]{0,2,1:T(8,128)(2,1)} %bitcast.14), calls=%async_computation.1 | async-start | bytes 4194304 | tf_op jit(solution)/shard_map/all_to_all | solution.py:18
  192.0 0.6 dynamic-slice
  193.3 75.2 %all-to-all-done = bf16[256,8,512]{0,2,1:T(8,128)(2,1)} async-done(((bf16[256,8,512]{0,2,1:T(8,128)(2,1)}), bf16[256,8,512]{0,2,1:T(8,128)(2,1)}, u32[]{:S(2)}, u32[]{:S(2)}) %all-to-all-start) | async-done | bytes 2097184 | tf_op jit(solution)/shard_map/all_to_all | solution.py:18
  268.5 3.9 %copy.12 = bf16[8,256,512]{2,1,0:T(8,128)(2,1)} copy(bf16[8,256,512]{1,2,0:T(8,128)(2,1)} %bitcast.2) | data formatting | bytes 4194304 | tf_op jit(solution)/shard_map/all_to_all | solution.py:18
  272.5 10.4 %all-reduce = f32[256]{0:T(256)} all-reduce(f32[256]{0:T(256)S(1)} %subtract_dynamic-update-slice_fusion), channel_id=1, replica_groups=mesh['dp'=4,'row'=2,'col'=4] {'col'}, use_global_device_ids=true, to_apply=%add | all-reduce | flops 256 | bytes 2048
  282.9 1.3 dynamic-slice_subtract_fusion
  284.2 6.7 %convolution_bitcast_fusion = f32[512,1024]{0,1:T(8,128)} fusion(bf16[2048,1024]{1,0:T(8,128)(2,1)} %all-gather.8.cloned.1.call-done, bf16[2048,512]{1,0:T(8,128)(2,1)} %bitcast.15), kind=kOutput, calls=%fused_computation.1 | convolution fusion | flops 2147483648 | bytes 8388608 | tf_op jit(solution)/shard_map/dot_general | solution.py:67
  290.9 2.9 copy.13
  293.8 20.2 %reduce-scatter.5.cloned.1.call-done = f32[1024,128]{1,0:T(8,128)} async-done(((f32[1024,1024]{1,0:T(8,128)}), f32[1024,128]{1,0:T(8,128)}) %reduce-scatter.5.cloned.1.call-update) | async-done | bytes 524304 | tf_op jit(solution)/shard_map/reduce_scatter | solution.py:66
  (36 shorter events, 0.7 us)
Async XLA Ops:
  8.0 31.3 %copy-start = (bf16[1024,1024]{1,0:T(8,128)(2,1)S(1)}, bf16[1024,1024]{1,0:T(8,128)(2,1)}, u32[]{:S(2)}) copy-start(bf16[1024,1024]{1,0:T(8,128)(2,1)} %param.7) | copy-start | bytes 6291460
  8.0 25.0 %all-gather.4.cloned.1.call-start = ((), (), s32[]{:S(2)}) async-start(), calls=%async_computation.3 | async-start | bytes 12582912 | tf_op jit(solution)/shard_map/all_gather | solution.py:25
  8.7 61.8 %reduce-scatter.3.cloned.1.call-start = ((), (), s32[]{:S(2)}) async-start(), calls=%async_computation.4 | async-start | bytes 1310720 | tf_op jit(solution)/shard_map/reduce_scatter | solution.py:29
  39.3 1.9 copy-start.2
  39.3 2.9 copy-start.5
  41.2 67.3 %all-gather.6.cloned.1.call-start = ((), (), s32[]{:S(2)}) async-start(), calls=%async_computation.5 | async-start | bytes 4325376 | tf_op jit(solution)/shard_map/all_gather | solution.py:23
  42.2 242.0 %all-gather.8.cloned.1.call-start = ((), (), s32[]{:S(2)}) async-start(), calls=%async_computation.6 | async-start | bytes 4718592 | tf_op jit(solution)/shard_map/all_gather | solution.py:64
  71.7 80.7 %copy-start.1 = (f32[64,1024]{1,0:T(8,128)S(1)}, f32[64,1024]{1,0:T(8,128)}, u32[]{:S(2)}) copy-start(f32[64,1024]{1,0:T(8,128)} %reduce-scatter.3.cloned.1.call-done) | copy-start | bytes 786436
  152.4 3.4 %copy-start.4 = (f32[2048]{0:T(1024)}, f32[2048]{0:T(1024)S(1)}, u32[]{:S(2)}) copy-start(f32[2048]{0:T(1024)S(1)} %get-tuple-element.21) | copy-start | bytes 24580
  155.9 6.6 %collective-permute-start = (bf16[64,1024]{1,0:T(8,128)(2,1)S(1)}, bf16[64,1024]{1,0:T(8,128)(2,1)S(1)}, u32[]{:S(2)}, u32[]{:S(2)}) collective-permute-start(bf16[64,1024]{1,0:T(8,128)(2,1)S(1)} %multiply_convert_fusion.1), channel_id=1, source_target_pairs={{0,1},{1,2},{2,3},{3,0},{4,5},{5,6},{6,7},{7,4},{8,9},{9,10},{10,1... | collective-permute-start | bytes 393224 | tf_op jit(solution)/shard_map/ppermute | solution.py:58
  162.5 6.0 %collective-permute-start.1 = (bf16[64,1024]{1,0:T(8,128)(2,1)S(1)}, bf16[64,1024]{1,0:T(8,128)(2,1)S(1)}, u32[]{:S(2)}, u32[]{:S(2)}) collective-permute-start(bf16[64,1024]{1,0:T(8,128)(2,1)S(1)} %collective-permute-done), channel_id=1, source_target_pairs={{0,1},{1,2},{2,3},{3,0},{4,5},{5,6},{6,7},{7,4},{8,9},{9,10},{10,1... | collective-permute-start | bytes 393224 | tf_op jit(solution)/shard_map/ppermute | solution.py:58
  168.4 6.0 %collective-permute-start.2 = (bf16[64,1024]{1,0:T(8,128)(2,1)S(1)}, bf16[64,1024]{1,0:T(8,128)(2,1)}, u32[]{:S(2)}, u32[]{:S(2)}) collective-permute-start(bf16[64,1024]{1,0:T(8,128)(2,1)S(1)} %collective-permute-done.1), channel_id=1, source_target_pairs={{0,1},{1,2},{2,3},{3,0},{4,5},{5,6},{6,7},{7,4},{8,9},{9,10},{10,1... | collective-permute-start | bytes 393224 | tf_op jit(solution)/shard_map/ppermute | solution.py:58
  176.3 1.0 copy-start.3
  179.4 134.5 %reduce-scatter.5.cloned.1.call-start = ((), (), s32[]{:S(2)}) async-start(), calls=%async_computation.7 | async-start | bytes 4718592 | tf_op jit(solution)/shard_map/reduce_scatter | solution.py:66
  187.5 4.5 %copy-start.6 = (u32[32]{0:T(128)S(1)}, u32[32]{0:T(128)}, u32[]{:S(2)}) copy-start(u32[32]{0:T(128)} %constant.71) | copy-start | bytes 388
  187.5 81.0 %all-to-all-start = ((bf16[256,8,512]{0,2,1:T(8,128)(2,1)}), bf16[256,8,512]{0,2,1:T(8,128)(2,1)}, u32[]{:S(2)}, u32[]{:S(2)}) async-start(bf16[256,8,512]{0,2,1:T(8,128)(2,1)} %bitcast.14), calls=%async_computation.1 | async-start | bytes 4194304 | tf_op jit(solution)/shard_map/all_to_all | solution.py:18
Sparse Core Ops, SparseCore 0:
  10.4 22.5 all-gather.3
  41.3 29.2 reduce-scatter.2
Sparse Core Ops, SparseCore 1:
  45.1 63.3 all-gather.5
  179.5 81.7 all-gather.7
  264.1 49.8 reduce-scatter.4
